TPU v7x, 32 devices: a whole 2x2x4 slice. The times are simulated.
32 devices in a mesh: rows: 4 (over y, core), cols: 8 (over z, x).
Axes of the slice: x: 2, y: 2, z: 4, core: 2. Of those that a mesh axis runs over, the one named last changes fastest.
Arguments:
- displacement: float32 [2048, 288], P(('rows', 'cols')), may hold values from -6 to 6
- positions: float32 [2048, 288], P(('rows', 'cols')), as said below
- cluster_basis: bfloat16 [2048, 288, 64], P(('rows', 'cols')), may hold values from -0.375 to 0.375
- near_pairs: int32 [8192, 2], P(('rows', 'cols')), may hold values from 0 to 67, as said below
- near_count: int32 [32], P(('rows', 'cols')), may hold values from 64 to 256, as said below
- far_pairs: int32 [32768, 2], P(('rows', 'cols')), may hold values from 0 to 511, as said below
- far_count: int32 [32], P(('rows', 'cols')), may hold values from 256 to 1024, as said below
- far_blocks: bfloat16 [32768, 64, 64], P(('rows', 'cols')), may hold values from -0.75 to 0.75
- intact: int32 [2048, 96], P(('rows', 'cols')), may hold values 0 or 1
- stiffness: float32 [2048, 96], P(('rows', 'cols')), may hold values from 0.5 to 2
Outputs:
- net_traction: float32 [2048, 288], P(('rows', 'cols'))
- damage: float32 [2048, 96], P(('rows', 'cols'))
Inputs may be any that keep to these rules, and one draw needn't show every extreme that they name: `positions`: centroids of the elements of each cluster. `near_pairs`: column 0 is a cluster of the device's own 64; column 1 counts from 2 clusters before the device's first cluster and names a cluster at most 2 away from the target in the cluster order. Dead slots hold valid entries too. `near_count`: loads differ from device to device. `far_pairs`: column 0 is a target cluster of the device's index along rows (0 to 511); column 1 a source cluster of its index along cols (0 to 255), numbered through the devices of that column in the order of rows. Dead slots hold valid entries too. `far_count`: loads differ from device to device.
All inputs are finite; a program needn't handle non-finite values. No bound on the sum of `intact` on one device may be relied on, other than what follows from the above.
Results may differ from a plain program's by a relative error of at most 0.0014.
Values may be sent and summed in bfloat16 or wider, within the bound.
No kernel may reach another device: no remote copies, remote signals or barrier semaphores. Data moves between devices by JAX's collectives and lax.ppermute only.
A program may use at most 128 MiB of HBM per device.

v0:
```python
import functools

import jax
import jax.numpy as jnp
from jax import lax
from jax.experimental import pallas as pl
from jax.experimental.pallas import tpu as pltpu
from jax.sharding import PartitionSpec as P

HALO = 2
LANES = 128
SUBLANES = 8
CHUNK = 32
GROUPS = LANES // CHUNK
core_square = 0.25
softening = 1.5
UNROLL = 8
FEW = 4
FOLD = 256
PIECES = 3
VMEM = 20 * 1024 * 1024


def split_rows(width, lanes):
    return pl.cdiv(width, lanes)


def in_hbm(count):
    return [pl.BlockSpec(memory_space=pltpu.HBM)] * count


def pinned(*arrays):
    return [pltpu.with_memory_space_constraint(x, pltpu.HBM) for x in arrays]


def start_all(sems, moves):
    copies = [
        pltpu.make_async_copy(source, target, sems.at[n])
        for n, (source, target) in enumerate(moves)
    ]
    for copy in copies:
        copy.start()
    return copies


def prepare_kernel(disp_hbm, pos_hbm, out_ref, halo_ref, disp_ref, pos_ref, sems):
    clusters, width = disp_ref.shape
    spare = halo_ref.shape[1]
    segments = split_rows(width, spare)
    copies = start_all(sems, ((disp_hbm, disp_ref), (pos_hbm, pos_ref)))
    halo_ref[...] = jnp.zeros_like(halo_ref)
    for copy in copies:
        copy.wait()
    out_ref[...] = disp_ref[...].astype(out_ref.dtype)
    row = 0
    for g in range(segments):
        size = min(spare, width - g * spare)
        for start in (0, clusters - HALO):
            for ref in (disp_ref, pos_ref):
                halo_ref[row : row + HALO, 0:size] = ref[
                    start : start + HALO, g * spare : g * spare + size
                ]
                row += HALO


def prepare(disp, pos, spare):
    clusters, width = disp.shape
    vmem = pl.BlockSpec(memory_space=pltpu.VMEM)
    return pl.pallas_call(
        prepare_kernel,
        out_shape=(
            jax.ShapeDtypeStruct((clusters, width), jnp.bfloat16),
            jax.ShapeDtypeStruct((clusters, spare), jnp.float32),
        ),
        in_specs=in_hbm(2),
        out_specs=(vmem, vmem),
        scratch_shapes=[
            pltpu.VMEM(disp.shape, disp.dtype),
            pltpu.VMEM(pos.shape, pos.dtype),
            pltpu.SemaphoreType.DMA((2,)),
        ],
        compiler_params=pltpu.CompilerParams(vmem_limit_bytes=VMEM),
        cost_estimate=pl.CostEstimate(
            flops=clusters * width, bytes_accessed=12 * clusters * width, transcendentals=0
        ),
        name="prepare",
    )(*pinned(disp, pos))


def far_kernel(
    count_hbm,
    pairs_hbm,
    gathered_hbm,
    blocks_ref,
    out_ref,
    count_ref,
    pairs_ref,
    gathered_ref,
    buffer,
    column_scr,
    coeff_scr,
    place_scr,
    sum_scr,
    summed_scr,
    halo_scr,
    sems,
    block_sems,
    *,
    segments,
):
    rank, _, slots = buffer.shape
    cols, clusters, _ = out_ref.shape
    targets = cols * clusters
    rows = gathered_ref.shape[0] // clusters
    sources = rows * clusters
    tiles = slots // FOLD

    def fetch(t):
        here = pl.ds(pl.multiple_of(t * FOLD, FOLD), FOLD)
        return pltpu.make_async_copy(
            blocks_ref.at[:, :, here], buffer.at[:, :, here], block_sems.at[t]
        )

    inputs = start_all(
        sems, ((count_hbm, count_ref), (pairs_hbm, pairs_ref), (gathered_hbm, gathered_ref))
    )
    fetch(0).start()
    summed_scr[...] = jnp.zeros_like(summed_scr)
    inputs[0].wait()
    count = count_ref[0]
    live = (count + FOLD - 1) // FOLD
    for t in range(1, tiles):

        @pl.when(t < live)
        def _(t=t):
            fetch(t).start()

    inputs[1].wait()
    inputs[2].wait()
    column_scr[...] = gathered_ref[...].astype(jnp.bfloat16)

    index = lax.broadcasted_iota(jnp.int32, (sources, slots), 0)
    pick = jnp.where(index == pairs_ref[1:2, :], 1.0, 0.0).astype(jnp.bfloat16)
    coeff = lax.dot_general(
        column_scr[...], pick, (((0,), (0,)), ((), ())), preferred_element_type=jnp.float32
    )
    coeff_scr[...] = coeff[0:rank, :]
    slot = lax.broadcasted_iota(jnp.int32, (1, slots), 1)
    wanted = jnp.where(slot < count, pairs_ref[0:1, :], -1)
    index = lax.broadcasted_iota(jnp.int32, (targets, slots), 0)
    place_scr[...] = jnp.where(index == wanted, 1.0, 0.0).astype(jnp.bfloat16)

    def multiply(t, carry):
        start = pl.multiple_of(t * FOLD, FOLD)
        lanes = pl.ds(start, FOLD)
        fetch(t).wait()
        coeff = coeff_scr[:, lanes]
        for r in range(rank):
            product = buffer[r, :, lanes].astype(jnp.float32) * coeff
            folded = product[0:SUBLANES]
            for s in range(1, rank // SUBLANES):
                folded = folded + product[s * SUBLANES : (s + 1) * SUBLANES]
            for h in range(FOLD // LANES):
                sum_scr[h, r * SUBLANES : (r + 1) * SUBLANES, :] = folded[
                    :, h * LANES : (h + 1) * LANES
                ]
        parts = []
        for h in range(FOLD // LANES):
            total = sum_scr[h, pl.ds(0, rank, stride=SUBLANES), :]
            for s in range(1, SUBLANES):
                total = total + sum_scr[h, pl.ds(s, rank, stride=SUBLANES), :]
            parts.append(total)
        coupled = jnp.concatenate(parts, axis=1)
        high = coupled.astype(jnp.bfloat16)
        low = (coupled - high.astype(jnp.float32)).astype(jnp.bfloat16)
        both = jnp.concatenate([high, low], axis=0)
        summed_scr[...] += lax.dot_general(
            place_scr[:, lanes], both, (((1,), (1,)), ((), ())), preferred_element_type=jnp.float32
        )
        return carry

    lax.fori_loop(0, live, multiply, 0)

    i = lax.axis_index("rows")
    j = lax.axis_index("cols")
    from_last = jnp.where(j < cols - 1, i, i - 1)
    from_first = jnp.where(j > 0, i, i + 1)
    edge = 2 * HALO
    halo_scr[...] = jnp.zeros_like(halo_scr)
    sides = (
        (0, jnp.minimum(from_first, rows - 1), from_first < rows),
        (edge, jnp.maximum(from_last, 0), from_last >= 0),
    )
    for side, (row, owner, there) in enumerate(sides):
        start = pl.multiple_of(owner * clusters, clusters)
        whole = jnp.where(there, gathered_ref[pl.ds(start, clusters), :], 0.0)
        for n in range(PIECES):
            piece = whole.astype(jnp.bfloat16).astype(jnp.float32)
            whole = whole - piece
            for g in range(segments):
                to = (n * segments + g) * edge
                here = g * 2 * edge + row
                halo_scr[side, to : to + edge, :] = piece[here : here + edge, :]
    after = jnp.where(j < cols - 1, j + 1, 0)
    lane = lax.broadcasted_iota(jnp.int32, (clusters, LANES), 1)
    for d in range(cols):
        halo = halo_scr[jnp.where(after == d, 1, 0)]
        mine = summed_scr[d * clusters : (d + 1) * clusters, :]
        mine = mine + pltpu.roll(mine, rank, 1)
        out_ref[d] = jnp.where(lane < rank, mine, halo).astype(out_ref.dtype)


def far_field(count, pairs, gathered, blocks, cols, segments):
    rank, _, slots = blocks.shape
    rows = lax.axis_size("rows")
    clusters = gathered.shape[0] // rows
    return pl.pallas_call(
        functools.partial(far_kernel, segments=segments),
        out_shape=jax.ShapeDtypeStruct((cols, clusters, LANES), jnp.bfloat16),
        in_specs=in_hbm(3) + [pl.BlockSpec(memory_space=pl.ANY)],
        out_specs=pl.BlockSpec(memory_space=pltpu.VMEM),
        scratch_shapes=[
            pltpu.SMEM(count.shape, count.dtype),
            pltpu.VMEM(pairs.shape, pairs.dtype),
            pltpu.VMEM(gathered.shape, gathered.dtype),
            pltpu.VMEM(blocks.shape, blocks.dtype),
            pltpu.VMEM((rows * clusters, LANES), jnp.bfloat16),
            pltpu.VMEM((rank, slots), jnp.float32),
            pltpu.VMEM((cols * clusters, slots), jnp.bfloat16),
            pltpu.VMEM((FOLD // LANES, rank * SUBLANES, LANES), jnp.float32),
            pltpu.VMEM((cols * clusters, LANES), jnp.float32),
            pltpu.VMEM((2, clusters, LANES), jnp.float32),
            pltpu.SemaphoreType.DMA((3,)),
            pltpu.SemaphoreType.DMA((slots // FOLD,)),
        ],
        compiler_params=pltpu.CompilerParams(vmem_limit_bytes=VMEM),
        cost_estimate=pl.CostEstimate(
            flops=2 * rank * rank * slots,
            bytes_accessed=2 * rank * rank * slots,
            transcendentals=0,
        ),
        name="far_field",
    )(count, *pinned(pairs), gathered, *pinned(blocks))


def replicate(rows, chunks, store, turned=False):
    within = lax.broadcasted_iota(jnp.int32, (rows.shape[0], LANES), 1)
    if turned:
        within = within + (within // CHUNK) * SUBLANES
    within = within % CHUNK
    for m in range(3 * chunks):
        tile = m // GROUPS
        store(
            m,
            jnp.take_along_axis(
                rows[:, tile * LANES : (tile + 1) * LANES],
                within + (m % GROUPS) * CHUNK,
                axis=1,
                mode="promise_in_bounds",
            ),
        )


def row_of(ref, n, row):
    return ref[n, pl.ds(row, SUBLANES, stride=0), :]


def turn(wide):
    return pltpu.roll(wide, 0, 1, stride=1, stride_axis=0)


def pair_sums(tgt, src, chunks):
    sums = [None] * (3 * chunks)
    size = 3 * chunks
    for f in range(chunks):
        y = [src(c * chunks + f) for c in range(3)]
        u = [src(size + c * chunks + f) for c in range(3)]
        v = [3.0 * x for x in u]
        for h in range(chunks):
            r = [tgt[c * chunks + h] - y[c] for c in range(3)]
            q = (r[0] * r[0] + core_square) + (r[1] * r[1] + r[2] * r[2])
            s = r[0] * v[0] + (r[1] * v[1] + r[2] * v[2])
            inverse = lax.rsqrt(q)
            square = inverse * inverse
            weight = square * inverse
            s = s * square
            for c in range(3):
                term = weight * (u[c] - s * r[c])
                m = c * chunks + h
                sums[m] = term if sums[m] is None else sums[m] + term
    return sums


def gather_sums(acc_scr, clusters, chunks, store):
    own_group = lax.broadcasted_iota(jnp.int32, (clusters, LANES), 1) // CHUNK
    for t in range(pl.cdiv(3 * chunks, GROUPS)):
        merged = None
        for g in range(GROUPS):
            m = t * GROUPS + g
            if m >= 3 * chunks:
                break
            total = acc_scr[m, pl.ds(0, clusters, stride=SUBLANES), :]
            for s in range(1, SUBLANES):
                total = total + acc_scr[m, pl.ds(s, clusters, stride=SUBLANES), :]
            total = total + pltpu.roll(total, 2 * CHUNK, 1)
            total = total + pltpu.roll(total, CHUNK, 1)
            merged = total if merged is None else jnp.where(own_group == g, total, merged)
        store(t, merged)


def turn_matrix():
    shape = (PIECES * CHUNK, SUBLANES * LANES)
    column = lax.broadcasted_iota(jnp.int32, shape, 1)
    lane = column % LANES
    entry = (lane + (lane // CHUNK) * SUBLANES + column // LANES) % CHUNK
    row = lax.broadcasted_iota(jnp.int32, shape, 0) % CHUNK
    return jnp.where(entry == row, 1.0, 0.0).astype(jnp.bfloat16)


def exact_pieces(value):
    pieces = []
    for _ in range(PIECES):
        piece = value.astype(jnp.bfloat16)
        pieces.append(piece)
        value = value - piece.astype(jnp.float32)
    return pieces


def near_kernel(
    pairs_hbm,
    count_hbm,
    disp_hbm,
    pos_hbm,
    intact_hbm,
    stiff_hbm,
    out_hbm,
    damage_hbm,
    rest_hbm,
    pairs_ref,
    count_ref,
    disp_ref,
    pos_ref,
    intact_ref,
    stiff_ref,
    out_ref,
    damage_ref,
    rest_ref,
    plan_ref,
    plan_smem,
    wide_scr,
    piece_scr,
    turn_scr,
    tgt_scr,
    src_scr,
    acc_scr,
    sems,
    out_sems,
    plan_sem,
):
    clusters, width = disp_ref.shape
    elems = width // 3
    chunks = elems // CHUNK
    size = 3 * chunks
    slots = pairs_ref.shape[1]

    inputs = start_all(
        sems,
        (
            (pos_hbm, pos_ref),
            (disp_hbm, disp_ref),
            (pairs_hbm, pairs_ref),
            (count_hbm, count_ref),
            (intact_hbm, intact_ref),
            (stiff_hbm, stiff_ref),
        ),
    )
    acc_scr[...] = jnp.zeros_like(acc_scr)
    turn_scr[...] = turn_matrix()
    for copy in inputs[2:4]:
        copy.wait()
    count = count_ref[0]

    target = pairs_ref[0:1, :]
    source = pairs_ref[1:2, :]
    live = lax.broadcasted_iota(jnp.int32, (1, slots), 1) < count
    own = jnp.logical_and(source >= HALO, source < clusters + HALO)
    plan_ref[0:1, :] = target
    plan_ref[1:2, :] = jnp.clip(source - HALO, 0, clusters - 1)
    plan_ref[2:3, :] = jnp.where(jnp.logical_and(live, own), target, clusters) * SUBLANES
    plan = pltpu.make_async_copy(plan_ref, plan_smem, plan_sem)
    plan.start()

    others = jnp.where(jnp.logical_and(live, jnp.logical_not(own)), 1.0, 0.0)
    square = (slots, slots)
    upto = lax.broadcasted_iota(jnp.int32, square, 0) <= lax.broadcasted_iota(jnp.int32, square, 1)
    upto = jnp.where(upto, 1.0, 0.0).astype(jnp.bfloat16)
    order = jnp.dot(
        jnp.broadcast_to(others, (SUBLANES, slots)).astype(jnp.bfloat16),
        upto,
        preferred_element_type=jnp.float32,
    )
    place = jnp.where(others > 0.0, order[0:1, :] - 1.0, -1.0).astype(jnp.int32)
    place = lax.broadcasted_iota(jnp.int32, square, 0) == place
    place = jnp.where(place, 1.0, 0.0).astype(jnp.bfloat16)
    row = lax.broadcasted_iota(jnp.int32, (SUBLANES, slots), 0)
    listed = jnp.where(row == 0, target, source).astype(jnp.float32).astype(jnp.bfloat16)
    listed = lax.dot_general(
        listed, place, (((1,), (1,)), ((), ())), preferred_element_type=jnp.float32
    )
    number = jnp.sum(others, axis=1, keepdims=True)
    rest_ref[...] = jnp.where(row < 2, listed, number).astype(jnp.int32)
    rest_out = pltpu.make_async_copy(rest_ref, rest_hbm, out_sems.at[1])
    rest_out.start()

    for k, values in enumerate((pos_ref, disp_ref)):
        inputs[k].wait()
        wide_scr[k, :, 0:width] = values[...]
        for m in range(size):
            pieces = exact_pieces(values[:, m * CHUNK : (m + 1) * CHUNK])
            piece_scr[(k * size + m) * clusters : (k * size + m + 1) * clusters, :] = (
                jnp.concatenate(pieces, axis=1)
            )
    columns = 2 * LANES
    for t in range(SUBLANES * LANES // columns):
        for k in range(2):
            rows = size * clusters
            turned = jnp.dot(
                piece_scr[k * rows : (k + 1) * rows, :],
                turn_scr[:, t * columns : (t + 1) * columns],
                preferred_element_type=jnp.float32,
            )
            for m in range(size):
                for h in range(columns // LANES):
                    s = t * (columns // LANES) + h
                    src_scr[k * size + m, pl.ds(s, clusters, stride=SUBLANES), :] = turned[
                        m * clusters : (m + 1) * clusters, h * LANES : (h + 1) * LANES
                    ]

    def store_target(m, value):
        tgt_scr[m] = value

    replicate(wide_scr[0], chunks, store_target)
    for copy in inputs[4:]:
        copy.wait()

    disp = [disp_ref[:, c * elems : (c + 1) * elems] for c in range(3)]
    separation = jnp.sqrt(1.0 + (disp[0] * disp[0] + disp[1] * disp[1] + disp[2] * disp[2]))
    softened = 1.0 - jnp.exp(-(separation - 1.0) / softening)
    intact = intact_ref[...].astype(jnp.float32)
    damage = intact * softened + (1.0 - intact)
    damage_ref[...] = damage
    damage_out = pltpu.make_async_copy(damage_ref, damage_hbm, out_sems.at[0])
    damage_out.start()
    hold = (1.0 - damage) * stiff_ref[...]
    for c in range(3):
        out_ref[:, c * elems : (c + 1) * elems] = -hold * disp[c]
    plan.wait()

    def one_pair(slot):
        target = plan_smem[0, slot]
        source = pl.multiple_of(plan_smem[1, slot] * SUBLANES, SUBLANES)
        into = pl.multiple_of(plan_smem[2, slot], SUBLANES)
        tgt = [row_of(tgt_scr, m, target) for m in range(size)]
        sums = pair_sums(tgt, lambda n: src_scr[n, pl.ds(source, SUBLANES), :], chunks)
        for m in range(size):
            acc_scr[m, pl.ds(into, SUBLANES), :] += sums[m]

    def step(it, carry):
        for k in range(UNROLL):
            one_pair(it * UNROLL + k)
        return carry

    lax.fori_loop(0, (count + UNROLL - 1) // UNROLL, step, 0)

    def store_sum(t, value):
        wide_scr[0, :, t * LANES : (t + 1) * LANES] = value

    gather_sums(acc_scr, clusters, chunks, store_sum)
    out_ref[...] += wide_scr[0, :, 0:width]
    near_out = pltpu.make_async_copy(out_ref, out_hbm, out_sems.at[2])
    near_out.start()
    for copy in (damage_out, rest_out, near_out):
        copy.wait()


def near_field(pairs, count, disp, pos, intact, stiffness):
    clusters, width = disp.shape
    elems = width // 3
    chunks = elems // CHUNK
    padded = pl.cdiv(width, LANES) * LANES
    slots = pairs.shape[1]
    return pl.pallas_call(
        near_kernel,
        out_shape=(
            jax.ShapeDtypeStruct((clusters, width), jnp.float32),
            jax.ShapeDtypeStruct((clusters, elems), jnp.float32),
            jax.ShapeDtypeStruct((SUBLANES, slots), jnp.int32),
        ),
        in_specs=in_hbm(6),
        out_specs=tuple(in_hbm(3)),
        scratch_shapes=[
            pltpu.VMEM(pairs.shape, pairs.dtype),
            pltpu.SMEM(count.shape, count.dtype),
            pltpu.VMEM(disp.shape, disp.dtype),
            pltpu.VMEM(pos.shape, pos.dtype),
            pltpu.VMEM(intact.shape, intact.dtype),
            pltpu.VMEM(stiffness.shape, stiffness.dtype),
            pltpu.VMEM((clusters, width), jnp.float32),
            pltpu.VMEM((clusters, elems), jnp.float32),
            pltpu.VMEM((SUBLANES, slots), jnp.int32),
            pltpu.VMEM((SUBLANES, slots), jnp.int32),
            pltpu.SMEM((SUBLANES, slots), jnp.int32),
            pltpu.VMEM((2, clusters, padded), jnp.float32),
            pltpu.VMEM((6 * chunks * clusters, PIECES * CHUNK), jnp.bfloat16),
            pltpu.VMEM((PIECES * CHUNK, SUBLANES * LANES), jnp.bfloat16),
            pltpu.VMEM((3 * chunks, clusters, LANES), jnp.float32),
            pltpu.VMEM((6 * chunks, clusters * SUBLANES, LANES), jnp.float32),
            pltpu.VMEM((3 * chunks, (clusters + 1) * SUBLANES, LANES), jnp.float32),
            pltpu.SemaphoreType.DMA((6,)),
            pltpu.SemaphoreType.DMA((3,)),
            pltpu.SemaphoreType.DMA(()),
        ],
        compiler_params=pltpu.CompilerParams(vmem_limit_bytes=VMEM),
        cost_estimate=pl.CostEstimate(
            flops=30 * slots * elems * elems,
            bytes_accessed=4 * clusters * width * 6,
            transcendentals=slots * elems * elems,
        ),
        name="near_field",
    )(*pinned(pairs), count, *pinned(disp, pos, intact, stiffness))


def finish_kernel(
    rest_hbm,
    pos_hbm,
    received_ref,
    near_ref,
    far_ref,
    out_ref,
    rest_ref,
    pos_ref,
    ext_scr,
    halo_scr,
    tgt_scr,
    src_scr,
    acc_scr,
    sems,
    *,
    rank,
):
    clusters, width = near_ref.shape
    cols = received_ref.shape[0]
    elems = width // 3
    chunks = elems // CHUNK
    size = 3 * chunks
    spare = LANES - rank
    segments = split_rows(width, spare)
    edge = 2 * HALO
    tail = pl.ds(clusters - SUBLANES, SUBLANES)

    inputs = start_all(
        sems,
        (
            (rest_hbm, rest_ref),
            (pos_hbm.at[pl.ds(0, SUBLANES)], pos_ref.at[0]),
            (pos_hbm.at[tail], pos_ref.at[1]),
        ),
    )
    acc_scr[...] = jnp.zeros_like(acc_scr)

    j = lax.axis_index("cols")
    before = jnp.where(j > 0, j - 1, cols - 1)
    after = jnp.where(j < cols - 1, j + 1, 0)
    for start, sender in ((0, before), (HALO, after)):
        halo_scr[...] = received_ref[sender].astype(jnp.float32)
        rows = edge * segments
        whole = halo_scr[0:rows, :]
        for n in range(1, PIECES):
            whole = whole + halo_scr[n * rows : (n + 1) * rows, :]
        for g in range(segments):
            count = min(spare, width - g * spare)
            for k in range(2):
                row = (2 * g + k) * HALO
                ext_scr[k, start : start + HALO, g * spare : g * spare + count] = whole[
                    row : row + HALO, rank : rank + count
                ]
    inputs[1].wait()
    inputs[2].wait()
    ext_scr[1, edge : edge + HALO, 0:width] = pos_ref[0, 0:HALO, :]
    ext_scr[1, edge + HALO : 2 * edge, 0:width] = pos_ref[1, SUBLANES - HALO :, :]
    for k in range(2):

        def store(m, value, k=k):
            for b in range(edge):
                wide = jnp.broadcast_to(value[b : b + 1, :], (SUBLANES, LANES))
                src_scr[(1 - k) * size + m, b * SUBLANES : (b + 1) * SUBLANES, :] = turn(wide)

        replicate(ext_scr[k], chunks, store, True)

    def store_target(m, value):
        tgt_scr[m] = value

    replicate(ext_scr[1], chunks, store_target)
    inputs[0].wait()
    number = rest_ref[2, 0]

    def one_pair(n):
        target = rest_ref[0, n]
        source = rest_ref[1, n]
        target = jnp.where(target < HALO, target, target - (clusters - edge))
        source = jnp.where(source < HALO, source, source - clusters)
        live = n < number
        target = jnp.where(live, target, edge)
        source = pl.multiple_of(jnp.where(live, source, 0) * SUBLANES, SUBLANES)
        into = pl.multiple_of(target * SUBLANES, SUBLANES)
        row = edge + jnp.where(live, target, 0)
        tgt = [row_of(tgt_scr, m, row) for m in range(size)]
        sums = pair_sums(tgt, lambda k: src_scr[k, pl.ds(source, SUBLANES), :], chunks)
        for m in range(size):
            acc_scr[m, pl.ds(into, SUBLANES), :] += sums[m]

    def step(it, carry):
        for k in range(FEW):
            one_pair(it * FEW + k)
        return carry

    lax.fori_loop(0, (number + FEW - 1) // FEW, step, 0)

    def store_sum(t, value):
        ext_scr[0, :, t * LANES : (t + 1) * LANES] = value

    gather_sums(acc_scr, 2 * edge, chunks, store_sum)
    out_ref[...] = near_ref[...] + far_ref[...]
    out_ref[0:HALO, :] += ext_scr[0, 0:HALO, 0:width]
    out_ref[clusters - HALO :, :] += ext_scr[0, HALO:edge, 0:width]


def finish(rest, pos, received, near, far, rank):
    clusters, width = pos.shape
    chunks = width // 3 // CHUNK
    padded = pl.cdiv(width, LANES) * LANES
    edge = 2 * HALO
    vmem = pl.BlockSpec(memory_space=pltpu.VMEM)
    return pl.pallas_call(
        functools.partial(finish_kernel, rank=rank),
        out_shape=jax.ShapeDtypeStruct((clusters, width), jnp.float32),
        in_specs=in_hbm(2) + [vmem] * 3,
        out_specs=vmem,
        scratch_shapes=[
            pltpu.SMEM(rest.shape, rest.dtype),
            pltpu.VMEM((2, SUBLANES, width), pos.dtype),
            pltpu.VMEM((2, 2 * edge, padded), jnp.float32),
            pltpu.VMEM((clusters, LANES), jnp.float32),
            pltpu.VMEM((3 * chunks, 2 * edge, LANES), jnp.float32),
            pltpu.VMEM((6 * chunks, edge * SUBLANES, LANES), jnp.float32),
            pltpu.VMEM((3 * chunks, 2 * edge * SUBLANES, LANES), jnp.float32),
            pltpu.SemaphoreType.DMA((3,)),
        ],
        compiler_params=pltpu.CompilerParams(vmem_limit_bytes=VMEM),
        cost_estimate=pl.CostEstimate(
            flops=2 * clusters * width, bytes_accessed=16 * clusters * width, transcendentals=0
        ),
        name="finish",
    )(rest, *pinned(pos), received, near, far)


def local(
    displacement,
    positions,
    cluster_basis,
    near_pairs,
    near_count,
    far_pairs,
    far_count,
    far_blocks,
    intact,
    stiffness,
):
    cols = lax.axis_size("cols")
    clusters, width, rank = cluster_basis.shape
    spare = LANES - rank
    segments = split_rows(width, spare)
    disp_bf, halo = prepare(displacement, positions, spare)
    coeff = jnp.einsum("kf,kfr->kr", disp_bf, cluster_basis, preferred_element_type=jnp.float32)
    payload = jnp.concatenate([coeff, halo], axis=1)
    gathered = lax.all_gather(payload, "rows", axis=0, tiled=True)
    partial = far_field(
        far_count, far_pairs.T, gathered, far_blocks.transpose(1, 2, 0), cols, segments
    )
    received = lax.all_to_all(partial, "cols", split_axis=0, concat_axis=0)
    near, damage, rest = near_field(
        near_pairs.T, near_count, displacement, positions, intact, stiffness
    )
    owned = jnp.sum(received[:, :, :rank].astype(jnp.float32), axis=0).astype(jnp.bfloat16)
    far = jnp.einsum("kfr,kr->kf", cluster_basis, owned, preferred_element_type=jnp.float32)
    return finish(rest, positions, received, near, far, rank), damage


def solution(mesh):
    both = ("rows", "cols")
    in_specs = (
        P(both, None),
        P(both, None),
        P(both, None, None),
        P(both, None),
        P(both),
        P(both, None),
        P(both),
        P(both, None, None),
        P(both, None),
        P(both, None),
    )
    out_specs = (P(both, None), P(both, None))
    return jax.shard_map(local, mesh=mesh, in_specs=in_specs, out_specs=out_specs, check_vma=False)
```

profile of v0, /device:TPU:3, one launch (start us, length us, event | category | flops | bytes accessed | tf_op | source)
XLA Modules:
  0.0 37.6 jit_solution(7639142463495406170)
XLA Ops:
  0.6 0.0 copy-start
  1.4 1.2 %prepare.1 = (bf16[64,288]{1,0:T(8,128)(2,1)S(1)}, f32[64,64]{1,0:T(8,128)S(1)}) custom-call(f32[64,288]{1,0:T(8,128)} %disp_hbm.3, f32[64,288]{1,0:T(8,128)} %pos_hbm.5), custom_call_target="tpu_custom_call" | custom-call | flops 18432 | bytes 221184 | tf_op jit(solution)/shard_map/prepare/pallas_call | solution.py:69
  2.6 0.0 copy-done
  2.7 1.2 %fusion = f32[64,1,64]{2,1,0:T(1,128)S(1)} fusion(bf16[64,288,64]{1,2,0:T(8,128)(2,1)S(1)} %copy-done, bf16[64,288,1]{1,0,2:T(8,128)(2,1)S(1)} %bitcast.13), kind=kOutput, calls=%fused_computation.2 | convolution fusion | flops 2359296 | bytes 2412544 | tf_op jit(solution)/shard_map/kf,kfr->kr/dot_general | solution.py:684
  3.8 0.1 pad_maximum_fusion
  3.9 5.9 %all_gather.3.gathered_hbm = f32[256,128]{1,0:T(8,128)S(1)} all-gather(f32[64,128]{1,0:T(8,128)S(1)} %pad_maximum_fusion), channel_id=1, replica_groups=mesh['rows'=4,'cols'=8] {'rows'}, dimensions={0}, use_global_device_ids=true | all-gather | bytes 163840 | tf_op jit(solution)/shard_map/all_gather | solution.py:686
  9.8 4.3 %far_field.1 = bf16[8,64,128]{2,1,0:T(8,128)(2,1)} custom-call(s32[1]{0:T(128)S(6)} %copy.23.count_hbm, s32[2,1024]{1,0:T(2,128)} %bitcast.17, f32[256,128]{1,0:T(8,128)S(1)} %all_gather.3.gathered_hbm, bf16[64,64,1024]{2,1,0:T(8,128)(2,1)} %bitcast.14), custom_call_target="tpu_custom_call" | custom-call | flops 8388608 | bytes 8388608 | tf_op jit(solution)/shard_map/far_field/pallas_call | solution.py:217
  14.1 6.5 %all-to-all-start = ((bf16[8,64,128]{2,1,0:T(8,128)(2,1)}), bf16[8,64,128]{2,1,0:T(8,128)(2,1)S(1)}, u32[]{:S(2)}, u32[]{:S(2)}) async-start(bf16[8,64,128]{2,1,0:T(8,128)(2,1)} %far_field.1), calls=%async_computation | async-start | bytes 262144 | tf_op jit(solution)/shard_map/all_to_all | solution.py:690
  21.3 13.2 %near_field.1 = (f32[64,288]{1,0:T(8,128)S(1)}, f32[64,96]{1,0:T(8,128)}, s32[8,256]{1,0:T(8,128)S(1)}) custom-call(s32[2,256]{1,0:T(2,128)} %bitcast.18, s32[1]{0:T(128)S(6)} %copy.22.count_hbm, f32[64,288]{1,0:T(8,128)} %disp_hbm.3, f32[64,288]{1,0:T(8,128)} %pos_hbm.5, s32[64,96]{1,0:T(8,128)} %intact_hbm.1, f32[64,96]{1,0:T(8,128)} %stiff_hbm.1), custom_call_target="tpu_custom_call" | custom-call | flops 70778880 | bytes 442368 | tf_op jit(solution)/shard_map/near_field/pallas_call | solution.py:492
  34.5 0.0 all-to-all-done.received_ref
  34.5 0.6 %fusion.2 = f32[64,1,288]{2,1,0:T(1,128)S(1)} fusion(bf16[64,288,64]{1,2,0:T(8,128)(2,1)S(1)} %copy-done, bf16[64,64,1]{1,0,2:T(8,128)(2,1)S(1)} %bitcast.15), kind=kOutput, calls=%fused_computation.5 | convolution fusion | flops 2359296 | bytes 2441216 | tf_op jit(solution)/shard_map/kfr,kr->kf/dot_general | solution.py:695
  35.2 2.4 %finish.1 = f32[64,288]{1,0:T(8,128)} custom-call(s32[8,256]{1,0:T(8,128)S(1)} %get-tuple-element.7.rest_hbm, f32[64,288]{1,0:T(8,128)} %pos_hbm.5, bf16[8,64,128]{2,1,0:T(8,128)(2,1)S(1)} %all-to-all-done.received_ref, f32[64,288]{1,0:T(8,128)S(1)} %get-tuple-element.10.near_ref, f32[64,288]{1,0:T(8,128)S(1)} %bitcast.12), custom_call_target="tpu_custom_call" | custom-call | flops 36864 | bytes 294912 | tf_op jit(solution)/shard_map/finish/pallas_call | solution.py:644
  (2 shorter events, 0.0 us)
Async XLA Ops:
  0.6 2.0 %copy-start = (bf16[64,288,64]{1,2,0:T(8,128)(2,1)S(1)}, bf16[64,288,64]{1,2,0:T(8,128)(2,1)}, u32[]{:S(2)}) copy-start(bf16[64,288,64]{1,2,0:T(8,128)(2,1)} %param.12) | copy-start | bytes 7077892
  14.1 20.4 %all-to-all-start = ((bf16[8,64,128]{2,1,0:T(8,128)(2,1)}), bf16[8,64,128]{2,1,0:T(8,128)(2,1)S(1)}, u32[]{:S(2)}, u32[]{:S(2)}) async-start(bf16[8,64,128]{2,1,0:T(8,128)(2,1)} %far_field.1), calls=%async_computation | async-start | bytes 262144 | tf_op jit(solution)/shard_map/all_to_all | solution.py:690
where the time goes:
time: 37.9 us; the launch traced here: 37.6 us
  Pallas kernels  21 us (55%)
  starting transfers between devices  6.55 us (17%)
  blocking collectives  5.93 us (16%)
  between operations  2.14 us (6%)
  matrix products  1.82 us (5%)
    pallas_call x1, Pallas kernels, near_field(): pl.pallas_call(near_kernel, out_shape=(jax.ShapeDtypeStruct((clusters, wi...  13.2 us
    all_to_all x1, starting transfers between devices, local(): received = lax.all_to_all(partial, 'cols', split_axis=0, concat_axis=0)  6.55 us
    all_gather x1, blocking collectives, local(): gathered = lax.all_gather(payload, 'rows', axis=0, tiled=True)  5.93 us
    pallas_call x1, Pallas kernels, far_field(): pl.pallas_call(functools.partial(far_kernel, segments=segments), out_shap...  4.26 us
    pallas_call x1, Pallas kernels, finish(): pl.pallas_call(functools.partial(finish_kernel, rank=rank), out_shape=jax...  2.4 us
    pallas_call x1, Pallas kernels, prepare(): pl.pallas_call(prepare_kernel, out_shape=(jax.ShapeDtypeStruct((clusters,...  1.19 us
    dot_general x1, matrix products, local(): jnp.einsum('kf,kfr->kr', disp_bf, cluster_basis, preferred_element_type=j...  1.18 us
  transfers between devices with their start and end apart: 1, of which 0 were waited for; matrix products, arithmetic and copies ran while one was open for 0% of the time, Pallas kernels for 35%

commit v1 on v0

--- a/solution.py
+++ b/solution.py
@@ -43,15 +43,45 @@
     return copies
 
 
-def prepare_kernel(disp_hbm, pos_hbm, out_ref, halo_ref, disp_ref, pos_ref, sems):
+def prepare_kernel(
+    near_count_ref,
+    far_count_ref,
+    pairs_hbm,
+    disp_hbm,
+    pos_hbm,
+    intact_hbm,
+    stiff_hbm,
+    low_ref,
+    halo_ref,
+    disp_ref,
+    pos_ref,
+    base_ref,
+    damage_ref,
+    list_ref,
+    pairs_ref,
+    intact_ref,
+    stiff_ref,
+    sems,
+):
     clusters, width = disp_ref.shape
+    elems = width // 3
     spare = halo_ref.shape[1]
     segments = split_rows(width, spare)
-    copies = start_all(sems, ((disp_hbm, disp_ref), (pos_hbm, pos_ref)))
+    inputs = start_all(
+        sems,
+        (
+            (pairs_hbm, pairs_ref),
+            (disp_hbm, disp_ref),
+            (pos_hbm, pos_ref),
+            (intact_hbm, intact_ref),
+            (stiff_hbm, stiff_ref),
+        ),
+    )
     halo_ref[...] = jnp.zeros_like(halo_ref)
-    for copy in copies:
+    for copy in inputs:
         copy.wait()
-    out_ref[...] = disp_ref[...].astype(out_ref.dtype)
+    list_pairs(pairs_ref, near_count_ref[0], far_count_ref[0], list_ref, clusters)
+    low_ref[...] = disp_ref[...].astype(low_ref.dtype)
     row = 0
     for g in range(segments):
         size = min(spare, width - g * spare)
@@ -62,38 +92,89 @@
                 ]
                 row += HALO
 
-
-def prepare(disp, pos, spare):
+    disp = [disp_ref[:, c * elems : (c + 1) * elems] for c in range(3)]
+    separation = jnp.sqrt(1.0 + (disp[0] * disp[0] + disp[1] * disp[1] + disp[2] * disp[2]))
+    softened = 1.0 - jnp.exp(-(separation - 1.0) / softening)
+    intact = intact_ref[...].astype(jnp.float32)
+    damage = intact * softened + (1.0 - intact)
+    damage_ref[...] = damage
+    hold = (1.0 - damage) * stiff_ref[...]
+    for c in range(3):
+        base_ref[:, c * elems : (c + 1) * elems] = -hold * disp[c]
+
+
+def list_pairs(pairs_ref, near_count, far_count, list_ref, clusters):
+    slots = pairs_ref.shape[1]
+    target = pairs_ref[0:1, :]
+    source = pairs_ref[1:2, :]
+    live = lax.broadcasted_iota(jnp.int32, (1, slots), 1) < near_count
+    own = jnp.logical_and(source >= HALO, source < clusters + HALO)
+    list_ref[0:1, :] = target
+    list_ref[1:2, :] = jnp.clip(source - HALO, 0, clusters - 1)
+    list_ref[2:3, :] = jnp.where(jnp.logical_and(live, own), target, clusters) * SUBLANES
+    list_ref[3:4, :] = jnp.full((1, slots), near_count, jnp.int32)
+    others = jnp.where(jnp.logical_and(live, jnp.logical_not(own)), 1.0, 0.0)
+    square = (slots, slots)
+    upto = lax.broadcasted_iota(jnp.int32, square, 0) <= lax.broadcasted_iota(jnp.int32, square, 1)
+    upto = jnp.where(upto, 1.0, 0.0).astype(jnp.bfloat16)
+    order = jnp.dot(
+        jnp.broadcast_to(others, (SUBLANES, slots)).astype(jnp.bfloat16),
+        upto,
+        preferred_element_type=jnp.float32,
+    )
+    place = jnp.where(others > 0.0, order[0:1, :] - 1.0, -1.0).astype(jnp.int32)
+    place = lax.broadcasted_iota(jnp.int32, square, 0) == place
+    place = jnp.where(place, 1.0, 0.0).astype(jnp.bfloat16)
+    row = lax.broadcasted_iota(jnp.int32, (SUBLANES, slots), 0)
+    listed = jnp.where(row == 0, target, source).astype(jnp.float32).astype(jnp.bfloat16)
+    listed = lax.dot_general(
+        listed, place, (((1,), (1,)), ((), ())), preferred_element_type=jnp.float32
+    ).astype(jnp.int32)
+    list_ref[4:6, :] = listed[0:2, :]
+    number = jnp.sum(others, axis=1, keepdims=True).astype(jnp.int32)
+    list_ref[6:7, :] = jnp.broadcast_to(number, (1, slots))
+    list_ref[7:8, :] = jnp.full((1, slots), far_count, jnp.int32)
+
+
+def prepare(near_count, far_count, pairs, disp, pos, intact, stiffness, spare):
     clusters, width = disp.shape
+    slots = pairs.shape[1]
     vmem = pl.BlockSpec(memory_space=pltpu.VMEM)
+    smem = pl.BlockSpec(memory_space=pltpu.SMEM)
     return pl.pallas_call(
         prepare_kernel,
         out_shape=(
             jax.ShapeDtypeStruct((clusters, width), jnp.bfloat16),
             jax.ShapeDtypeStruct((clusters, spare), jnp.float32),
+            jax.ShapeDtypeStruct((clusters, width), jnp.float32),
+            jax.ShapeDtypeStruct((clusters, width), jnp.float32),
+            jax.ShapeDtypeStruct((clusters, width), jnp.float32),
+            jax.ShapeDtypeStruct(stiffness.shape, jnp.float32),
+            jax.ShapeDtypeStruct((SUBLANES, slots), jnp.int32),
         ),
-        in_specs=in_hbm(2),
-        out_specs=(vmem, vmem),
+        in_specs=[smem] * 2 + in_hbm(5),
+        out_specs=(vmem,) * 7,
         scratch_shapes=[
-            pltpu.VMEM(disp.shape, disp.dtype),
-            pltpu.VMEM(pos.shape, pos.dtype),
-            pltpu.SemaphoreType.DMA((2,)),
+            pltpu.VMEM(pairs.shape, pairs.dtype),
+            pltpu.VMEM(intact.shape, intact.dtype),
+            pltpu.VMEM(stiffness.shape, stiffness.dtype),
+            pltpu.SemaphoreType.DMA((5,)),
         ],
         compiler_params=pltpu.CompilerParams(vmem_limit_bytes=VMEM),
         cost_estimate=pl.CostEstimate(
-            flops=clusters * width, bytes_accessed=12 * clusters * width, transcendentals=0
+            flops=20 * clusters * width, bytes_accessed=24 * clusters * width, transcendentals=0
         ),
         name="prepare",
-    )(*pinned(disp, pos))
+    )(near_count, far_count, *pinned(pairs, disp, pos, intact, stiffness))
 
 
 def far_kernel(
-    count_hbm,
+    list_hbm,
     pairs_hbm,
     gathered_hbm,
     blocks_ref,
     out_ref,
-    count_ref,
+    list_ref,
     pairs_ref,
     gathered_ref,
     buffer,
@@ -122,12 +203,12 @@
         )
 
     inputs = start_all(
-        sems, ((count_hbm, count_ref), (pairs_hbm, pairs_ref), (gathered_hbm, gathered_ref))
+        sems, ((list_hbm, list_ref), (pairs_hbm, pairs_ref), (gathered_hbm, gathered_ref))
     )
     fetch(0).start()
     summed_scr[...] = jnp.zeros_like(summed_scr)
     inputs[0].wait()
-    count = count_ref[0]
+    count = list_ref[7, 0]
     live = (count + FOLD - 1) // FOLD
     for t in range(1, tiles):
 
@@ -210,7 +291,7 @@
         out_ref[d] = jnp.where(lane < rank, mine, halo).astype(out_ref.dtype)
 
 
-def far_field(count, pairs, gathered, blocks, cols, segments):
+def far_field(listed, pairs, gathered, blocks, cols, segments):
     rank, _, slots = blocks.shape
     rows = lax.axis_size("rows")
     clusters = gathered.shape[0] // rows
@@ -220,7 +301,7 @@
         in_specs=in_hbm(3) + [pl.BlockSpec(memory_space=pl.ANY)],
         out_specs=pl.BlockSpec(memory_space=pltpu.VMEM),
         scratch_shapes=[
-            pltpu.SMEM(count.shape, count.dtype),
+            pltpu.SMEM(listed.shape, listed.dtype),
             pltpu.VMEM(pairs.shape, pairs.dtype),
             pltpu.VMEM(gathered.shape, gathered.dtype),
             pltpu.VMEM(blocks.shape, blocks.dtype),
@@ -240,7 +321,7 @@
             transcendentals=0,
         ),
         name="far_field",
-    )(count, *pinned(pairs), gathered, *pinned(blocks))
+    )(listed, *pinned(pairs), gathered, *pinned(blocks))
 
 
 def replicate(rows, chunks, store, turned=False):
@@ -327,26 +408,14 @@
 
 
 def near_kernel(
-    pairs_hbm,
-    count_hbm,
-    disp_hbm,
-    pos_hbm,
-    intact_hbm,
-    stiff_hbm,
-    out_hbm,
-    damage_hbm,
-    rest_hbm,
-    pairs_ref,
-    count_ref,
+    list_hbm,
     disp_ref,
     pos_ref,
-    intact_ref,
-    stiff_ref,
+    base_ref,
+    damage_ref,
     out_ref,
-    damage_ref,
-    rest_ref,
-    plan_ref,
-    plan_smem,
+    damage_hbm,
+    list_ref,
     wide_scr,
     piece_scr,
     turn_scr,
@@ -354,66 +423,17 @@
     src_scr,
     acc_scr,
     sems,
-    out_sems,
-    plan_sem,
 ):
     clusters, width = disp_ref.shape
     elems = width // 3
     chunks = elems // CHUNK
     size = 3 * chunks
-    slots = pairs_ref.shape[1]
-
-    inputs = start_all(
-        sems,
-        (
-            (pos_hbm, pos_ref),
-            (disp_hbm, disp_ref),
-            (pairs_hbm, pairs_ref),
-            (count_hbm, count_ref),
-            (intact_hbm, intact_ref),
-            (stiff_hbm, stiff_ref),
-        ),
-    )
+
+    moves = start_all(sems, ((list_hbm, list_ref), (damage_ref, damage_hbm)))
     acc_scr[...] = jnp.zeros_like(acc_scr)
     turn_scr[...] = turn_matrix()
-    for copy in inputs[2:4]:
-        copy.wait()
-    count = count_ref[0]
-
-    target = pairs_ref[0:1, :]
-    source = pairs_ref[1:2, :]
-    live = lax.broadcasted_iota(jnp.int32, (1, slots), 1) < count
-    own = jnp.logical_and(source >= HALO, source < clusters + HALO)
-    plan_ref[0:1, :] = target
-    plan_ref[1:2, :] = jnp.clip(source - HALO, 0, clusters - 1)
-    plan_ref[2:3, :] = jnp.where(jnp.logical_and(live, own), target, clusters) * SUBLANES
-    plan = pltpu.make_async_copy(plan_ref, plan_smem, plan_sem)
-    plan.start()
-
-    others = jnp.where(jnp.logical_and(live, jnp.logical_not(own)), 1.0, 0.0)
-    square = (slots, slots)
-    upto = lax.broadcasted_iota(jnp.int32, square, 0) <= lax.broadcasted_iota(jnp.int32, square, 1)
-    upto = jnp.where(upto, 1.0, 0.0).astype(jnp.bfloat16)
-    order = jnp.dot(
-        jnp.broadcast_to(others, (SUBLANES, slots)).astype(jnp.bfloat16),
-        upto,
-        preferred_element_type=jnp.float32,
-    )
-    place = jnp.where(others > 0.0, order[0:1, :] - 1.0, -1.0).astype(jnp.int32)
-    place = lax.broadcasted_iota(jnp.int32, square, 0) == place
-    place = jnp.where(place, 1.0, 0.0).astype(jnp.bfloat16)
-    row = lax.broadcasted_iota(jnp.int32, (SUBLANES, slots), 0)
-    listed = jnp.where(row == 0, target, source).astype(jnp.float32).astype(jnp.bfloat16)
-    listed = lax.dot_general(
-        listed, place, (((1,), (1,)), ((), ())), preferred_element_type=jnp.float32
-    )
-    number = jnp.sum(others, axis=1, keepdims=True)
-    rest_ref[...] = jnp.where(row < 2, listed, number).astype(jnp.int32)
-    rest_out = pltpu.make_async_copy(rest_ref, rest_hbm, out_sems.at[1])
-    rest_out.start()
 
     for k, values in enumerate((pos_ref, disp_ref)):
-        inputs[k].wait()
         wide_scr[k, :, 0:width] = values[...]
         for m in range(size):
             pieces = exact_pieces(values[:, m * CHUNK : (m + 1) * CHUNK])
@@ -440,26 +460,13 @@
         tgt_scr[m] = value
 
     replicate(wide_scr[0], chunks, store_target)
-    for copy in inputs[4:]:
-        copy.wait()
-
-    disp = [disp_ref[:, c * elems : (c + 1) * elems] for c in range(3)]
-    separation = jnp.sqrt(1.0 + (disp[0] * disp[0] + disp[1] * disp[1] + disp[2] * disp[2]))
-    softened = 1.0 - jnp.exp(-(separation - 1.0) / softening)
-    intact = intact_ref[...].astype(jnp.float32)
-    damage = intact * softened + (1.0 - intact)
-    damage_ref[...] = damage
-    damage_out = pltpu.make_async_copy(damage_ref, damage_hbm, out_sems.at[0])
-    damage_out.start()
-    hold = (1.0 - damage) * stiff_ref[...]
-    for c in range(3):
-        out_ref[:, c * elems : (c + 1) * elems] = -hold * disp[c]
-    plan.wait()
+    moves[0].wait()
+    count = list_ref[3, 0]
 
     def one_pair(slot):
-        target = plan_smem[0, slot]
-        source = pl.multiple_of(plan_smem[1, slot] * SUBLANES, SUBLANES)
-        into = pl.multiple_of(plan_smem[2, slot], SUBLANES)
+        target = list_ref[0, slot]
+        source = pl.multiple_of(list_ref[1, slot] * SUBLANES, SUBLANES)
+        into = pl.multiple_of(list_ref[2, slot], SUBLANES)
         tgt = [row_of(tgt_scr, m, target) for m in range(size)]
         sums = pair_sums(tgt, lambda n: src_scr[n, pl.ds(source, SUBLANES), :], chunks)
         for m in range(size):
@@ -476,49 +483,34 @@
         wide_scr[0, :, t * LANES : (t + 1) * LANES] = value
 
     gather_sums(acc_scr, clusters, chunks, store_sum)
-    out_ref[...] += wide_scr[0, :, 0:width]
-    near_out = pltpu.make_async_copy(out_ref, out_hbm, out_sems.at[2])
-    near_out.start()
-    for copy in (damage_out, rest_out, near_out):
-        copy.wait()
-
-
-def near_field(pairs, count, disp, pos, intact, stiffness):
+    out_ref[...] = base_ref[...] + wide_scr[0, :, 0:width]
+    moves[1].wait()
+
+
+def near_field(listed, disp, pos, base, damage):
     clusters, width = disp.shape
     elems = width // 3
     chunks = elems // CHUNK
     padded = pl.cdiv(width, LANES) * LANES
-    slots = pairs.shape[1]
+    slots = listed.shape[1]
+    vmem = pl.BlockSpec(memory_space=pltpu.VMEM)
     return pl.pallas_call(
         near_kernel,
         out_shape=(
             jax.ShapeDtypeStruct((clusters, width), jnp.float32),
-            jax.ShapeDtypeStruct((clusters, elems), jnp.float32),
-            jax.ShapeDtypeStruct((SUBLANES, slots), jnp.int32),
+            jax.ShapeDtypeStruct(damage.shape, jnp.float32),
         ),
-        in_specs=in_hbm(6),
-        out_specs=tuple(in_hbm(3)),
+        in_specs=in_hbm(1) + [vmem] * 4,
+        out_specs=(vmem, *in_hbm(1)),
         scratch_shapes=[
-            pltpu.VMEM(pairs.shape, pairs.dtype),
-            pltpu.SMEM(count.shape, count.dtype),
-            pltpu.VMEM(disp.shape, disp.dtype),
-            pltpu.VMEM(pos.shape, pos.dtype),
-            pltpu.VMEM(intact.shape, intact.dtype),
-            pltpu.VMEM(stiffness.shape, stiffness.dtype),
-            pltpu.VMEM((clusters, width), jnp.float32),
-            pltpu.VMEM((clusters, elems), jnp.float32),
-            pltpu.VMEM((SUBLANES, slots), jnp.int32),
-            pltpu.VMEM((SUBLANES, slots), jnp.int32),
-            pltpu.SMEM((SUBLANES, slots), jnp.int32),
+            pltpu.SMEM(listed.shape, listed.dtype),
             pltpu.VMEM((2, clusters, padded), jnp.float32),
             pltpu.VMEM((6 * chunks * clusters, PIECES * CHUNK), jnp.bfloat16),
             pltpu.VMEM((PIECES * CHUNK, SUBLANES * LANES), jnp.bfloat16),
             pltpu.VMEM((3 * chunks, clusters, LANES), jnp.float32),
             pltpu.VMEM((6 * chunks, clusters * SUBLANES, LANES), jnp.float32),
             pltpu.VMEM((3 * chunks, (clusters + 1) * SUBLANES, LANES), jnp.float32),
-            pltpu.SemaphoreType.DMA((6,)),
-            pltpu.SemaphoreType.DMA((3,)),
-            pltpu.SemaphoreType.DMA(()),
+            pltpu.SemaphoreType.DMA((2,)),
         ],
         compiler_params=pltpu.CompilerParams(vmem_limit_bytes=VMEM),
         cost_estimate=pl.CostEstimate(
@@ -527,7 +519,7 @@
             transcendentals=slots * elems * elems,
         ),
         name="near_field",
-    )(*pinned(pairs), count, *pinned(disp, pos, intact, stiffness))
+    )(listed, disp, pos, base, damage)
 
 
 def finish_kernel(
@@ -602,11 +594,11 @@
 
     replicate(ext_scr[1], chunks, store_target)
     inputs[0].wait()
-    number = rest_ref[2, 0]
+    number = rest_ref[6, 0]
 
     def one_pair(n):
-        target = rest_ref[0, n]
-        source = rest_ref[1, n]
+        target = rest_ref[4, n]
+        source = rest_ref[5, n]
         target = jnp.where(target < HALO, target, target - (clusters - edge))
         source = jnp.where(source < HALO, source, source - clusters)
         live = n < number
@@ -680,20 +672,20 @@
     clusters, width, rank = cluster_basis.shape
     spare = LANES - rank
     segments = split_rows(width, spare)
-    disp_bf, halo = prepare(displacement, positions, spare)
+    disp_bf, halo, disp, pos, base, damage, listed = prepare(
+        near_count, far_count, near_pairs.T, displacement, positions, intact, stiffness, spare
+    )
     coeff = jnp.einsum("kf,kfr->kr", disp_bf, cluster_basis, preferred_element_type=jnp.float32)
     payload = jnp.concatenate([coeff, halo], axis=1)
     gathered = lax.all_gather(payload, "rows", axis=0, tiled=True)
     partial = far_field(
-        far_count, far_pairs.T, gathered, far_blocks.transpose(1, 2, 0), cols, segments
+        listed, far_pairs.T, gathered, far_blocks.transpose(1, 2, 0), cols, segments
     )
     received = lax.all_to_all(partial, "cols", split_axis=0, concat_axis=0)
-    near, damage, rest = near_field(
-        near_pairs.T, near_count, displacement, positions, intact, stiffness
-    )
+    near, damage = near_field(listed, disp, pos, base, damage)
     owned = jnp.sum(received[:, :, :rank].astype(jnp.float32), axis=0).astype(jnp.bfloat16)
     far = jnp.einsum("kfr,kr->kf", cluster_basis, owned, preferred_element_type=jnp.float32)
-    return finish(rest, positions, received, near, far, rank), damage
+    return finish(listed, positions, received, near, far, rank), damage
 
 
 def solution(mesh):

time: 37.9 us -> 39.3 us (1.037)
  the two profiles are of different devices: /device:TPU:3 before, /device:TPU:17 now
where the time goes in v1:
time: 39.3 us; the launch traced here: 38.8 us
  Pallas kernels  20.3 us (52%)
  starting transfers between devices  6.46 us (16%)
  blocking collectives  5.93 us (15%)
  between operations  2.31 us (6%)
  matrix products  1.82 us (5%)
  local copies, waits for them, and re-layouts  1.81 us (5%)
    pallas_call x1, Pallas kernels, near_field(): pl.pallas_call(near_kernel, out_shape=(jax.ShapeDtypeStruct((clusters, wi...  11.7 us
    all_to_all x1, starting transfers between devices, local(): received = lax.all_to_all(partial, 'cols', split_axis=0, concat_axis=0)  6.46 us
    all_gather x1, blocking collectives, local(): gathered = lax.all_gather(payload, 'rows', axis=0, tiled=True)  5.93 us
    pallas_call x1, Pallas kernels, far_field(): pl.pallas_call(functools.partial(far_kernel, segments=segments), out_shap...  5.1 us
    pallas_call x1, Pallas kernels, finish(): pl.pallas_call(functools.partial(finish_kernel, rank=rank), out_shape=jax...  2.24 us
    unnamed x10, local copies, waits for them, and re-layouts  1.8 us
    pallas_call x1, Pallas kernels, prepare(): pl.pallas_call(prepare_kernel, out_shape=(jax.ShapeDtypeStruct((clusters,...  1.35 us
    dot_general x1, matrix products, local(): jnp.einsum('kf,kfr->kr', disp_bf, cluster_basis, preferred_element_type=j...  1.18 us
  transfers between devices with their start and end apart: 1, of which 0 were waited for; matrix products, arithmetic and copies ran while one was open for 0% of the time, Pallas kernels for 30%

profile of v1, /device:TPU:17, one launch (start us, length us, event | category | flops | bytes accessed | tf_op | source)
XLA Modules:
  0.0 38.8 jit_solution(9723227374133274620)
XLA Ops:
  0.6 0.0 copy-start
  2.2 1.3 %prepare.1 = (bf16[64,288]{1,0:T(8,128)(2,1)S(1)}, f32[64,64]{1,0:T(8,128)S(1)}, f32[64,288]{1,0:T(8,128)S(1)}, f32[64,288]{1,0:T(8,128)S(1)}, f32[64,288]{1,0:T...) custom-call(s32[1]{0:T(128)S(6)} %copy.22.near_count_ref, s32[1]{0:T(128)S(6)} %copy.23.far_count_ref, ...), custom_call_target="tpu_custom_call" | custom-call | flops 368640 | bytes 442368 | tf_op jit(solution)/shard_map/prepare/pallas_call | solution.py:144
  3.6 0.0 copy-start.1
  3.6 0.0 copy-start.3
  3.6 0.0 copy-done
  3.6 1.2 %fusion = f32[64,1,64]{2,1,0:T(1,128)S(1)} fusion(bf16[64,288,64]{1,2,0:T(8,128)(2,1)S(1)} %copy-done, bf16[64,288,1]{1,0,2:T(8,128)(2,1)S(1)} %bitcast.13), kind=kOutput, calls=%fused_computation.2 | convolution fusion | flops 2359296 | bytes 2412544 | tf_op jit(solution)/shard_map/kf,kfr->kr/dot_general | solution.py:678
  4.8 0.0 copy-done.1
  4.8 0.1 pad_maximum_fusion
  4.9 0.0 copy-done.3
  4.9 5.9 %all_gather.3.gathered_hbm = f32[256,128]{1,0:T(8,128)S(1)} all-gather(f32[64,128]{1,0:T(8,128)S(1)} %pad_maximum_fusion), channel_id=1, replica_groups=mesh['rows'=4,'cols'=8] {'rows'}, dimensions={0}, use_global_device_ids=true | all-gather | bytes 163840 | tf_op jit(solution)/shard_map/all_gather | solution.py:680
  10.8 5.1 %far_field.1 = bf16[8,64,128]{2,1,0:T(8,128)(2,1)} custom-call(s32[8,256]{1,0:T(8,128)S(1)} %get-tuple-element.11.list_hbm.rest_hbm, s32[2,1024]{1,0:T(2,128)} %bitcast.17, f32[256,128]{1,0:T(8,128)S(1)} %all_gather.3.gathered_hbm, bf16[64,64,1024]{2,1,0:T(8,128)(2,1)} %bitcast.14), custom_call_target="tpu_custom_call" | custom-call | flops 8388608 | bytes 8388608 | tf_op jit(solution)/shard_map/far_field/pallas_call | solution.py:298
  15.9 6.5 %all-to-all-start = ((bf16[8,64,128]{2,1,0:T(8,128)(2,1)}), bf16[8,64,128]{2,1,0:T(8,128)(2,1)S(1)}, u32[]{:S(2)}, u32[]{:S(2)}) async-start(bf16[8,64,128]{2,1,0:T(8,128)(2,1)} %far_field.1), calls=%async_computation | async-start | bytes 262144 | tf_op jit(solution)/shard_map/all_to_all | solution.py:684
  22.4 0.0 copy-start.2
  22.4 0.9 %copy-done.2 = f32[64,288]{1,0:T(8,128)S(1)} copy-done((f32[64,288]{1,0:T(8,128)S(1)}, f32[64,288]{1,0:T(8,128)}, u32[]{:S(2)}) %copy-start.2) | copy-done | bytes 73752
  23.3 0.0 copy-start.4
  23.3 0.9 %copy-done.4 = f32[64,288]{1,0:T(8,128)S(1)} copy-done((f32[64,288]{1,0:T(8,128)S(1)}, f32[64,288]{1,0:T(8,128)}, u32[]{:S(2)}) %copy-start.4) | copy-done | bytes 73752
  24.2 11.7 %near_field.1 = (f32[64,288]{1,0:T(8,128)S(1)}, f32[64,96]{1,0:T(8,128)}) custom-call(s32[8,256]{1,0:T(8,128)S(1)} %get-tuple-element.11.list_hbm.rest_hbm, f32[64,288]{1,0:T(8,128)S(1)} %get-tuple-element.14.disp_ref, f32[64,288]{1,0:T(8,128)S(1)} %copy-done.2, f32[64,288]{1,0:T(8,128)S(1)} %copy-done.4, f32[64,96]{1,0:T(8,128)S(1)} %get-tuple-element.17.damage_ref), custom_call_target="tpu_custom_call" | custom-call | flops 70778880 | bytes 442368 | tf_op jit(solution)/shard_map/near_field/pallas_call | solution.py:497
  35.9 0.0 all-to-all-done.received_ref
  35.9 0.6 %fusion.2 = f32[64,1,288]{2,1,0:T(1,128)S(1)} fusion(bf16[64,288,64]{1,2,0:T(8,128)(2,1)S(1)} %copy-done, bf16[64,64,1]{1,0,2:T(8,128)(2,1)S(1)} %bitcast.15), kind=kOutput, calls=%fused_computation.5 | convolution fusion | flops 2359296 | bytes 2441216 | tf_op jit(solution)/shard_map/kfr,kr->kf/dot_general | solution.py:687
  36.6 2.2 %finish.1 = f32[64,288]{1,0:T(8,128)} custom-call(s32[8,256]{1,0:T(8,128)S(1)} %get-tuple-element.11.list_hbm.rest_hbm, f32[64,288]{1,0:T(8,128)} %pos_hbm.3, bf16[8,64,128]{2,1,0:T(8,128)(2,1)S(1)} %all-to-all-done.received_ref, f32[64,288]{1,0:T(8,128)S(1)} %get-tuple-element.18.near_ref, f32[64,288]{1,0:T(8,128)S(1)} %bitcast.12), custom_call_target="tpu_custom_call" | custom-call | flops 36864 | bytes 294912 | tf_op jit(solution)/shard_map/finish/pallas_call | solution.py:636
  (2 shorter events, 0.0 us)
Async XLA Ops:
  0.6 3.0 %copy-start = (bf16[64,288,64]{1,2,0:T(8,128)(2,1)S(1)}, bf16[64,288,64]{1,2,0:T(8,128)(2,1)}, u32[]{:S(2)}) copy-start(bf16[64,288,64]{1,2,0:T(8,128)(2,1)} %param.12) | copy-start | bytes 7077892
  3.6 1.2 %copy-start.1 = (f32[64,288]{1,0:T(8,128)}, f32[64,288]{1,0:T(8,128)S(1)}, u32[]{:S(2)}) copy-start(f32[64,288]{1,0:T(8,128)S(1)} %get-tuple-element.15.pos_ref) | copy-start | bytes 221188
  3.6 1.3 %copy-start.3 = (f32[64,288]{1,0:T(8,128)}, f32[64,288]{1,0:T(8,128)S(1)}, u32[]{:S(2)}) copy-start(f32[64,288]{1,0:T(8,128)S(1)} %get-tuple-element.16.base_ref) | copy-start | bytes 221188
  15.9 19.9 %all-to-all-start = ((bf16[8,64,128]{2,1,0:T(8,128)(2,1)}), bf16[8,64,128]{2,1,0:T(8,128)(2,1)S(1)}, u32[]{:S(2)}, u32[]{:S(2)}) async-start(bf16[8,64,128]{2,1,0:T(8,128)(2,1)} %far_field.1), calls=%async_computation | async-start | bytes 262144 | tf_op jit(solution)/shard_map/all_to_all | solution.py:684
  22.4 0.9 %copy-start.2 = (f32[64,288]{1,0:T(8,128)S(1)}, f32[64,288]{1,0:T(8,128)}, u32[]{:S(2)}) copy-start(f32[64,288]{1,0:T(8,128)} %copy-done.1) | copy-start | bytes 221188
  23.3 0.9 %copy-start.4 = (f32[64,288]{1,0:T(8,128)S(1)}, f32[64,288]{1,0:T(8,128)}, u32[]{:S(2)}) copy-start(f32[64,288]{1,0:T(8,128)} %copy-done.3) | copy-start | bytes 221188

commit v2 on v1

--- a/solution.py
+++ b/solution.py
@@ -49,22 +49,15 @@
     pairs_hbm,
     disp_hbm,
     pos_hbm,
-    intact_hbm,
-    stiff_hbm,
     low_ref,
     halo_ref,
+    list_ref,
+    pairs_ref,
     disp_ref,
     pos_ref,
-    base_ref,
-    damage_ref,
-    list_ref,
-    pairs_ref,
-    intact_ref,
-    stiff_ref,
     sems,
 ):
     clusters, width = disp_ref.shape
-    elems = width // 3
     spare = halo_ref.shape[1]
     segments = split_rows(width, spare)
     inputs = start_all(
@@ -73,8 +66,6 @@
             (pairs_hbm, pairs_ref),
             (disp_hbm, disp_ref),
             (pos_hbm, pos_ref),
-            (intact_hbm, intact_ref),
-            (stiff_hbm, stiff_ref),
         ),
     )
     halo_ref[...] = jnp.zeros_like(halo_ref)
@@ -91,16 +82,6 @@
                     start : start + HALO, g * spare : g * spare + size
                 ]
                 row += HALO
-
-    disp = [disp_ref[:, c * elems : (c + 1) * elems] for c in range(3)]
-    separation = jnp.sqrt(1.0 + (disp[0] * disp[0] + disp[1] * disp[1] + disp[2] * disp[2]))
-    softened = 1.0 - jnp.exp(-(separation - 1.0) / softening)
-    intact = intact_ref[...].astype(jnp.float32)
-    damage = intact * softened + (1.0 - intact)
-    damage_ref[...] = damage
-    hold = (1.0 - damage) * stiff_ref[...]
-    for c in range(3):
-        base_ref[:, c * elems : (c + 1) * elems] = -hold * disp[c]
 
 
 def list_pairs(pairs_ref, near_count, far_count, list_ref, clusters):
@@ -136,7 +117,7 @@
     list_ref[7:8, :] = jnp.full((1, slots), far_count, jnp.int32)
 
 
-def prepare(near_count, far_count, pairs, disp, pos, intact, stiffness, spare):
+def prepare(near_count, far_count, pairs, disp, pos, spare):
     clusters, width = disp.shape
     slots = pairs.shape[1]
     vmem = pl.BlockSpec(memory_space=pltpu.VMEM)
@@ -146,26 +127,22 @@
         out_shape=(
             jax.ShapeDtypeStruct((clusters, width), jnp.bfloat16),
             jax.ShapeDtypeStruct((clusters, spare), jnp.float32),
-            jax.ShapeDtypeStruct((clusters, width), jnp.float32),
-            jax.ShapeDtypeStruct((clusters, width), jnp.float32),
-            jax.ShapeDtypeStruct((clusters, width), jnp.float32),
-            jax.ShapeDtypeStruct(stiffness.shape, jnp.float32),
             jax.ShapeDtypeStruct((SUBLANES, slots), jnp.int32),
         ),
-        in_specs=[smem] * 2 + in_hbm(5),
-        out_specs=(vmem,) * 7,
+        in_specs=[smem] * 2 + in_hbm(3),
+        out_specs=(vmem,) * 3,
         scratch_shapes=[
             pltpu.VMEM(pairs.shape, pairs.dtype),
-            pltpu.VMEM(intact.shape, intact.dtype),
-            pltpu.VMEM(stiffness.shape, stiffness.dtype),
-            pltpu.SemaphoreType.DMA((5,)),
+            pltpu.VMEM(disp.shape, disp.dtype),
+            pltpu.VMEM(pos.shape, pos.dtype),
+            pltpu.SemaphoreType.DMA((3,)),
         ],
         compiler_params=pltpu.CompilerParams(vmem_limit_bytes=VMEM),
         cost_estimate=pl.CostEstimate(
             flops=20 * clusters * width, bytes_accessed=24 * clusters * width, transcendentals=0
         ),
         name="prepare",
-    )(near_count, far_count, *pinned(pairs, disp, pos, intact, stiffness))
+    )(near_count, far_count, *pinned(pairs, disp, pos))
 
 
 def far_kernel(
@@ -353,18 +330,17 @@
 def pair_sums(tgt, src, chunks):
     sums = [None] * (3 * chunks)
     size = 3 * chunks
-    for f in range(chunks):
-        y = [src(c * chunks + f) for c in range(3)]
-        u = [src(size + c * chunks + f) for c in range(3)]
-        v = [3.0 * x for x in u]
-        for h in range(chunks):
-            r = [tgt[c * chunks + h] - y[c] for c in range(3)]
+    for h in range(chunks):
+        x = [tgt(c * chunks + h) for c in range(3)]
+        for f in range(chunks):
+            r = [x[c] - src(c * chunks + f) for c in range(3)]
+            u = [src(size + c * chunks + f) for c in range(3)]
             q = (r[0] * r[0] + core_square) + (r[1] * r[1] + r[2] * r[2])
-            s = r[0] * v[0] + (r[1] * v[1] + r[2] * v[2])
+            s = r[0] * u[0] + (r[1] * u[1] + r[2] * u[2])
             inverse = lax.rsqrt(q)
             square = inverse * inverse
             weight = square * inverse
-            s = s * square
+            s = (3.0 * s) * square
             for c in range(3):
                 term = weight * (u[c] - s * r[c])
                 m = c * chunks + h
@@ -409,13 +385,18 @@
 
 def near_kernel(
     list_hbm,
-    disp_ref,
-    pos_ref,
-    base_ref,
-    damage_ref,
+    disp_hbm,
+    pos_hbm,
+    intact_hbm,
+    stiff_hbm,
     out_ref,
     damage_hbm,
     list_ref,
+    disp_ref,
+    pos_ref,
+    intact_ref,
+    stiff_ref,
+    damage_ref,
     wide_scr,
     piece_scr,
     turn_scr,
@@ -423,17 +404,28 @@
     src_scr,
     acc_scr,
     sems,
+    out_sem,
 ):
     clusters, width = disp_ref.shape
     elems = width // 3
     chunks = elems // CHUNK
     size = 3 * chunks
 
-    moves = start_all(sems, ((list_hbm, list_ref), (damage_ref, damage_hbm)))
+    inputs = start_all(
+        sems,
+        (
+            (pos_hbm, pos_ref),
+            (disp_hbm, disp_ref),
+            (intact_hbm, intact_ref),
+            (stiff_hbm, stiff_ref),
+            (list_hbm, list_ref),
+        ),
+    )
     acc_scr[...] = jnp.zeros_like(acc_scr)
     turn_scr[...] = turn_matrix()
 
     for k, values in enumerate((pos_ref, disp_ref)):
+        inputs[k].wait()
         wide_scr[k, :, 0:width] = values[...]
         for m in range(size):
             pieces = exact_pieces(values[:, m * CHUNK : (m + 1) * CHUNK])
@@ -460,15 +452,31 @@
         tgt_scr[m] = value
 
     replicate(wide_scr[0], chunks, store_target)
-    moves[0].wait()
+    for copy in inputs[2:]:
+        copy.wait()
     count = list_ref[3, 0]
+
+    disp = [disp_ref[:, c * elems : (c + 1) * elems] for c in range(3)]
+    separation = jnp.sqrt(1.0 + (disp[0] * disp[0] + disp[1] * disp[1] + disp[2] * disp[2]))
+    softened = 1.0 - jnp.exp(-(separation - 1.0) / softening)
+    intact = intact_ref[...].astype(jnp.float32)
+    damage = intact * softened + (1.0 - intact)
+    damage_ref[...] = damage
+    damage_out = pltpu.make_async_copy(damage_ref, damage_hbm, out_sem)
+    damage_out.start()
+    hold = (1.0 - damage) * stiff_ref[...]
+    for c in range(3):
+        out_ref[:, c * elems : (c + 1) * elems] = -hold * disp[c]
 
     def one_pair(slot):
         target = list_ref[0, slot]
         source = pl.multiple_of(list_ref[1, slot] * SUBLANES, SUBLANES)
         into = pl.multiple_of(list_ref[2, slot], SUBLANES)
-        tgt = [row_of(tgt_scr, m, target) for m in range(size)]
-        sums = pair_sums(tgt, lambda n: src_scr[n, pl.ds(source, SUBLANES), :], chunks)
+        sums = pair_sums(
+            lambda m: row_of(tgt_scr, m, target),
+            lambda n: src_scr[n, pl.ds(source, SUBLANES), :],
+            chunks,
+        )
         for m in range(size):
             acc_scr[m, pl.ds(into, SUBLANES), :] += sums[m]
 
@@ -483,11 +491,11 @@
         wide_scr[0, :, t * LANES : (t + 1) * LANES] = value
 
     gather_sums(acc_scr, clusters, chunks, store_sum)
-    out_ref[...] = base_ref[...] + wide_scr[0, :, 0:width]
-    moves[1].wait()
-
-
-def near_field(listed, disp, pos, base, damage):
+    out_ref[...] += wide_scr[0, :, 0:width]
+    damage_out.wait()
+
+
+def near_field(listed, disp, pos, intact, stiffness):
     clusters, width = disp.shape
     elems = width // 3
     chunks = elems // CHUNK
@@ -498,19 +506,25 @@
         near_kernel,
         out_shape=(
             jax.ShapeDtypeStruct((clusters, width), jnp.float32),
-            jax.ShapeDtypeStruct(damage.shape, jnp.float32),
-        ),
-        in_specs=in_hbm(1) + [vmem] * 4,
+            jax.ShapeDtypeStruct(stiffness.shape, jnp.float32),
+        ),
+        in_specs=in_hbm(5),
         out_specs=(vmem, *in_hbm(1)),
         scratch_shapes=[
             pltpu.SMEM(listed.shape, listed.dtype),
+            pltpu.VMEM(disp.shape, disp.dtype),
+            pltpu.VMEM(pos.shape, pos.dtype),
+            pltpu.VMEM(intact.shape, intact.dtype),
+            pltpu.VMEM(stiffness.shape, stiffness.dtype),
+            pltpu.VMEM(stiffness.shape, jnp.float32),
             pltpu.VMEM((2, clusters, padded), jnp.float32),
             pltpu.VMEM((6 * chunks * clusters, PIECES * CHUNK), jnp.bfloat16),
             pltpu.VMEM((PIECES * CHUNK, SUBLANES * LANES), jnp.bfloat16),
             pltpu.VMEM((3 * chunks, clusters, LANES), jnp.float32),
             pltpu.VMEM((6 * chunks, clusters * SUBLANES, LANES), jnp.float32),
             pltpu.VMEM((3 * chunks, (clusters + 1) * SUBLANES, LANES), jnp.float32),
-            pltpu.SemaphoreType.DMA((2,)),
+            pltpu.SemaphoreType.DMA((5,)),
+            pltpu.SemaphoreType.DMA(()),
         ],
         compiler_params=pltpu.CompilerParams(vmem_limit_bytes=VMEM),
         cost_estimate=pl.CostEstimate(
@@ -519,7 +533,7 @@
             transcendentals=slots * elems * elems,
         ),
         name="near_field",
-    )(listed, disp, pos, base, damage)
+    )(listed, *pinned(disp, pos, intact, stiffness))
 
 
 def finish_kernel(
@@ -606,8 +620,11 @@
         source = pl.multiple_of(jnp.where(live, source, 0) * SUBLANES, SUBLANES)
         into = pl.multiple_of(target * SUBLANES, SUBLANES)
         row = edge + jnp.where(live, target, 0)
-        tgt = [row_of(tgt_scr, m, row) for m in range(size)]
-        sums = pair_sums(tgt, lambda k: src_scr[k, pl.ds(source, SUBLANES), :], chunks)
+        sums = pair_sums(
+            lambda m: row_of(tgt_scr, m, row),
+            lambda k: src_scr[k, pl.ds(source, SUBLANES), :],
+            chunks,
+        )
         for m in range(size):
             acc_scr[m, pl.ds(into, SUBLANES), :] += sums[m]
 
@@ -672,8 +689,8 @@
     clusters, width, rank = cluster_basis.shape
     spare = LANES - rank
     segments = split_rows(width, spare)
-    disp_bf, halo, disp, pos, base, damage, listed = prepare(
-        near_count, far_count, near_pairs.T, displacement, positions, intact, stiffness, spare
+    disp_bf, halo, listed = prepare(
+        near_count, far_count, near_pairs.T, displacement, positions, spare
     )
     coeff = jnp.einsum("kf,kfr->kr", disp_bf, cluster_basis, preferred_element_type=jnp.float32)
     payload = jnp.concatenate([coeff, halo], axis=1)
@@ -682,7 +699,7 @@
         listed, far_pairs.T, gathered, far_blocks.transpose(1, 2, 0), cols, segments
     )
     received = lax.all_to_all(partial, "cols", split_axis=0, concat_axis=0)
-    near, damage = near_field(listed, disp, pos, base, damage)
+    near, damage = near_field(listed, displacement, positions, intact, stiffness)
     owned = jnp.sum(received[:, :, :rank].astype(jnp.float32), axis=0).astype(jnp.bfloat16)
     far = jnp.einsum("kfr,kr->kf", cluster_basis, owned, preferred_element_type=jnp.float32)
     return finish(listed, positions, received, near, far, rank), damage

time: 39.3 us -> 38.6 us (0.982)
  the two profiles are of different devices: /device:TPU:17 before, /device:TPU:7 now
where the time goes in v2:
time: 38.6 us; the launch traced here: 38 us
  Pallas kernels  21.1 us (55%)
  starting transfers between devices  6.66 us (17%)
  blocking collectives  5.93 us (15%)
  between operations  2.29 us (6%)
  matrix products  1.82 us (5%)
    pallas_call x1, Pallas kernels, near_field(): pl.pallas_call(near_kernel, out_shape=(jax.ShapeDtypeStruct((clusters, wi...  12.5 us
    all_to_all x1, starting transfers between devices, local(): received = lax.all_to_all(partial, 'cols', split_axis=0, concat_axis=0)  6.66 us
    all_gather x1, blocking collectives, local(): gathered = lax.all_gather(payload, 'rows', axis=0, tiled=True)  5.93 us
    pallas_call x1, Pallas kernels, far_field(): pl.pallas_call(functools.partial(far_kernel, segments=segments), out_shap...  5.09 us
    pallas_call x1, Pallas kernels, finish(): pl.pallas_call(functools.partial(finish_kernel, rank=rank), out_shape=jax...  2.24 us
    pallas_call x1, Pallas kernels, prepare(): pl.pallas_call(prepare_kernel, out_shape=(jax.ShapeDtypeStruct((clusters,...  1.32 us
    dot_general x1, matrix products, local(): jnp.einsum('kf,kfr->kr', disp_bf, cluster_basis, preferred_element_type=j...  1.18 us
  transfers between devices with their start and end apart: 1, of which 0 were waited for; matrix products, arithmetic and copies ran while one was open for 0% of the time, Pallas kernels for 33%

profile of v2, /device:TPU:7, one launch (start us, length us, event | category | flops | bytes accessed | tf_op | source)
XLA Modules:
  0.0 38.0 jit_solution(2154147571321333507)
XLA Ops:
  0.6 0.0 copy-start
  2.2 1.3 %prepare.1 = (bf16[64,288]{1,0:T(8,128)(2,1)S(1)}, f32[64,64]{1,0:T(8,128)S(1)}, s32[8,256]{1,0:T(8,128)S(1)}) custom-call(s32[1]{0:T(128)S(6)} %copy.22.near_count_ref, s32[1]{0:T(128)S(6)} %copy.23.far_count_ref, s32[2,256]{1,0:T(2,128)} %bitcast.18, f32[64,288]{1,0:T(8,128)} %disp_hbm.3, f32[64,288]{1,0:T(8,128)} %pos_hbm.5), custom_call_target="tpu_custom_call" | custom-call | flops 368640 | bytes 442368 | tf_op jit(solution)/shard_map/prepare/pallas_call | solution.py:125
  3.6 0.0 copy-done
  3.6 1.2 %fusion = f32[64,1,64]{2,1,0:T(1,128)S(1)} fusion(bf16[64,288,64]{1,2,0:T(8,128)(2,1)S(1)} %copy-done, bf16[64,288,1]{1,0,2:T(8,128)(2,1)S(1)} %bitcast.13), kind=kOutput, calls=%fused_computation.2 | convolution fusion | flops 2359296 | bytes 2412544 | tf_op jit(solution)/shard_map/kf,kfr->kr/dot_general | solution.py:695
  4.8 0.1 pad_maximum_fusion
  4.9 5.9 %all_gather.3.gathered_hbm = f32[256,128]{1,0:T(8,128)S(1)} all-gather(f32[64,128]{1,0:T(8,128)S(1)} %pad_maximum_fusion), channel_id=1, replica_groups=mesh['rows'=4,'cols'=8] {'rows'}, dimensions={0}, use_global_device_ids=true | all-gather | bytes 163840 | tf_op jit(solution)/shard_map/all_gather | solution.py:697
  10.8 5.1 %far_field.1 = bf16[8,64,128]{2,1,0:T(8,128)(2,1)} custom-call(s32[8,256]{1,0:T(8,128)S(1)} %get-tuple-element.7.list_hbm.rest_hbm, s32[2,1024]{1,0:T(2,128)} %bitcast.17, f32[256,128]{1,0:T(8,128)S(1)} %all_gather.3.gathered_hbm, bf16[64,64,1024]{2,1,0:T(8,128)(2,1)} %bitcast.14), custom_call_target="tpu_custom_call" | custom-call | flops 8388608 | bytes 8388608 | tf_op jit(solution)/shard_map/far_field/pallas_call | solution.py:275
  15.9 6.7 %all-to-all-start = ((bf16[8,64,128]{2,1,0:T(8,128)(2,1)}), bf16[8,64,128]{2,1,0:T(8,128)(2,1)S(1)}, u32[]{:S(2)}, u32[]{:S(2)}) async-start(bf16[8,64,128]{2,1,0:T(8,128)(2,1)} %far_field.1), calls=%async_computation | async-start | bytes 262144 | tf_op jit(solution)/shard_map/all_to_all | solution.py:701
  22.5 12.5 %near_field.1 = (f32[64,288]{1,0:T(8,128)S(1)}, f32[64,96]{1,0:T(8,128)}) custom-call(s32[8,256]{1,0:T(8,128)S(1)} %get-tuple-element.7.list_hbm.rest_hbm, f32[64,288]{1,0:T(8,128)} %disp_hbm.3, f32[64,288]{1,0:T(8,128)} %pos_hbm.5, s32[64,96]{1,0:T(8,128)} %intact_hbm.1, f32[64,96]{1,0:T(8,128)} %stiff_hbm.1), custom_call_target="tpu_custom_call" | custom-call | flops 70778880 | bytes 442368 | tf_op jit(solution)/shard_map/near_field/pallas_call | solution.py:505
  35.0 0.0 all-to-all-done.received_ref
  35.1 0.6 %fusion.2 = f32[64,1,288]{2,1,0:T(1,128)S(1)} fusion(bf16[64,288,64]{1,2,0:T(8,128)(2,1)S(1)} %copy-done, bf16[64,64,1]{1,0,2:T(8,128)(2,1)S(1)} %bitcast.15), kind=kOutput, calls=%fused_computation.5 | convolution fusion | flops 2359296 | bytes 2441216 | tf_op jit(solution)/shard_map/kfr,kr->kf/dot_general | solution.py:704
  35.8 2.2 %finish.1 = f32[64,288]{1,0:T(8,128)} custom-call(s32[8,256]{1,0:T(8,128)S(1)} %get-tuple-element.7.list_hbm.rest_hbm, f32[64,288]{1,0:T(8,128)} %pos_hbm.5, bf16[8,64,128]{2,1,0:T(8,128)(2,1)S(1)} %all-to-all-done.received_ref, f32[64,288]{1,0:T(8,128)S(1)} %get-tuple-element.10.near_ref, f32[64,288]{1,0:T(8,128)S(1)} %bitcast.12), custom_call_target="tpu_custom_call" | custom-call | flops 36864 | bytes 294912 | tf_op jit(solution)/shard_map/finish/pallas_call | solution.py:653
  (2 shorter events, 0.0 us)
Async XLA Ops:
  0.6 2.9 %copy-start = (bf16[64,288,64]{1,2,0:T(8,128)(2,1)S(1)}, bf16[64,288,64]{1,2,0:T(8,128)(2,1)}, u32[]{:S(2)}) copy-start(bf16[64,288,64]{1,2,0:T(8,128)(2,1)} %param.12) | copy-start | bytes 7077892
  15.9 19.2 %all-to-all-start = ((bf16[8,64,128]{2,1,0:T(8,128)(2,1)}), bf16[8,64,128]{2,1,0:T(8,128)(2,1)S(1)}, u32[]{:S(2)}, u32[]{:S(2)}) async-start(bf16[8,64,128]{2,1,0:T(8,128)(2,1)} %far_field.1), calls=%async_computation | async-start | bytes 262144 | tf_op jit(solution)/shard_map/all_to_all | solution.py:701
